TPU v7x, 256 devices: a whole 4x4x8 slice. The times are simulated.
256 devices in a mesh: chan: 32 (over y, x, core), win: 8 (over z).
Axes of the slice: x: 4, y: 4, z: 8, core: 2. Of those that a mesh axis runs over, the one named last changes fastest.
Arguments:
- traces: bfloat16 [48, 8192, 1024], P('win', 'chan'), may hold values from -200 to 200
- offsets: int32 [32, 3], replicated, may hold values from -3 to 3, as said below
- counts: int32 [32], replicated, may hold values from 1 to 3, as said below
Outputs:
- correlations: float32 [96, 256, 1024], P('chan', 'win')
Inputs may be any that keep to these rules, and one draw needn't show every extreme that they name: Each row o holds 3 distinct nonzero offsets, and o + offsets[o, p] names a block, 0 to 31. `counts`: at least one owner has all 3 slots live.
All inputs are finite; a program needn't handle non-finite values.
Results may differ from a plain program's by a relative error of at most 0.0052.
Values may be sent and summed in bfloat16 or wider, within the bound.
A program may use at most 128 MiB of HBM per device.

v0:
```python
import functools
import math

import jax
import jax.numpy as jnp
from jax import lax
from jax.sharding import PartitionSpec as P

RADIUS = 8
MAXOFF = 3
PAIRS_DEV = 3


WATER = 0.8
EPS = 1e-06


def from_behind(value, axis, steps):
    count = lax.axis_size(axis)
    first, last = (max(0, -steps), min(count, count - steps))
    return lax.ppermute(value, axis, [(source, source + steps) for source in range(first, last)])


def band_layout(half_rows, groups):
    band_width = half_rows // groups
    spectral_rows = jnp.arange(2 * half_rows, dtype=jnp.int32)
    part_im = spectral_rows // band_width % 2
    frequency = spectral_rows // (2 * band_width) * band_width + spectral_rows % band_width
    return (frequency, part_im)


def angles_of(length, frequency):
    samples_axis = jnp.arange(length, dtype=jnp.int32)
    phase_index = samples_axis[:, None] * frequency[None, :] % length
    return phase_index.astype(jnp.float32) * (2.0 * math.pi / length)


def forward_table(length, groups):
    frequency, part_im = band_layout(length // 2, groups)
    angles = angles_of(length, frequency)
    return jnp.where(part_im[None, :] == 0, jnp.cos(angles), -jnp.sin(angles)).astype(jnp.bfloat16)


def inverse_table(length, groups):
    frequency, part_im = band_layout(length // 2, groups)
    angles = angles_of(length, frequency).T
    return jnp.where(part_im[:, None] == 0, jnp.cos(angles), -jnp.sin(angles))


def whiten(spectra, groups):
    segments, spectral_rows, channels = spectra.shape
    half_rows = spectral_rows // 2
    band_width = half_rows // groups
    layout = spectra.reshape(segments, groups, 2, band_width, channels)
    real_part = layout[:, :, 0].reshape(segments, half_rows, channels)
    imag_part = layout[:, :, 1].reshape(segments, half_rows, channels)
    amplitude = jnp.sqrt(real_part * real_part + imag_part * imag_part)
    windowed = lax.reduce_window(
        amplitude,
        jnp.zeros((), amplitude.dtype),
        lax.add,
        (1, 2 * RADIUS + 1, 1),
        (1, 1, 1),
        ((0, 0), (RADIUS, RADIUS), (0, 0)),
    )
    frequency = jnp.arange(half_rows, dtype=jnp.int32)
    bin_count = (
        jnp.minimum(frequency + RADIUS, half_rows - 1) - jnp.maximum(frequency - RADIUS, 0) + 1
    ).astype(amplitude.dtype)
    smooth = windowed / bin_count[None, :, None]
    water_level = WATER * jnp.mean(amplitude, axis=1, keepdims=True) + EPS
    divisor = jnp.maximum(smooth, water_level)
    real_white = (real_part / divisor).reshape(segments, groups, band_width, channels)
    imag_white = (imag_part / divisor).reshape(segments, groups, band_width, channels)
    whitened = jnp.stack([real_white, imag_white], axis=2)
    return whitened.reshape(segments, spectral_rows, channels).astype(jnp.bfloat16)


def cross_terms(source_real, source_imag, receiver_real, receiver_imag, sum_axis):
    real_sum = jnp.sum(source_real * receiver_real + source_imag * receiver_imag, axis=sum_axis)
    imag_sum = jnp.sum(source_real * receiver_imag - source_imag * receiver_real, axis=sum_axis)
    return (real_sum, imag_sum)


def cross_pair(source, receiver, groups):
    segments, spectral_rows, channels = source.shape
    band_width = spectral_rows // (2 * groups)
    source_view = source.reshape(segments, groups, 2, band_width, channels)
    receiver_view = receiver.reshape(segments, groups, 2, band_width, channels)
    real_sum, imag_sum = cross_terms(
        source_view[:, :, 0].astype(jnp.float32),
        source_view[:, :, 1].astype(jnp.float32),
        receiver_view[:, :, 0].astype(jnp.float32),
        receiver_view[:, :, 1].astype(jnp.float32),
        0,
    )
    return jnp.stack([real_sum, imag_sum], axis=1).reshape(spectral_rows, channels)


def return_piece(piece):
    return piece


def body(traces, offsets, counts):
    groups = lax.axis_size("chan")
    win_size = lax.axis_size("win")
    segments, channels, length = traces.shape
    half_rows = length // 2
    dft_table = forward_table(length, groups)
    spectra = jnp.einsum("sct,tk->skc", traces, dft_table, preferred_element_type=jnp.float32)
    whitened = whiten(spectra, groups)
    owner_index = lax.axis_index("chan")
    own_offsets = lax.dynamic_index_in_dim(offsets, owner_index, 0, keepdims=False)
    own_count = lax.dynamic_index_in_dim(counts, owner_index, 0, keepdims=False)
    forward_list = []
    backward_list = []
    for distance in range(1, MAXOFF + 1):
        forward_list.append(from_behind(whitened, "chan", -distance))
        backward_list.append(from_behind(whitened, "chan", distance))
    nearby = backward_list[::-1] + forward_list
    branches = [functools.partial(return_piece, piece) for piece in nearby]

    def add_pair(slot_index, totals):
        offset_now = own_offsets[slot_index]
        choose = jnp.where(offset_now < 0, offset_now + MAXOFF, offset_now + MAXOFF - 1)
        remote = lax.switch(choose, branches)
        product = cross_pair(whitened, remote, groups)
        return lax.dynamic_update_index_in_dim(totals, product, slot_index, 0)

    start_totals = jnp.zeros((PAIRS_DEV, 2 * half_rows, channels), jnp.float32)
    totals = lax.fori_loop(0, own_count, add_pair, start_totals)
    stacked = lax.psum_scatter(totals, "win", scatter_dimension=2, tiled=True)
    inverse = inverse_table(length, groups)
    norm_factor = 1.0 / math.sqrt(half_rows * segments * win_size)
    correlations = jnp.einsum(
        "pkc,kt->pct",
        stacked,
        inverse,
        precision=lax.Precision.HIGHEST,
        preferred_element_type=jnp.float32,
    )
    return correlations * norm_factor


def solution(mesh):
    in_specs = (P("win", "chan", None), P(), P())
    out_specs = P("chan", "win", None)
    return jax.shard_map(body, mesh=mesh, in_specs=in_specs, out_specs=out_specs, check_vma=False)
```

profile of v0, /device:TPU:1, one launch (start us, length us, event | category | flops | bytes accessed | tf_op | source)
XLA Modules:
  0.0 512.6 jit_solution(7127498438806168763)
XLA Ops:
  6.5 0.0 copy-start
  6.5 0.0 all-reduce.3.cloned.1.call-start
  6.6 1.9 copy-done
  8.4 19.4 %fusion.25 = f32[1024,6,256]{2,0,1:T(8,128)S(1)} fusion(bf16[6,256,1024]{2,1,0:T(8,128)(2,1)S(1)} %copy-done, s32[1024]{0:T(1024)S(1)} %fusion.53, pred[1024]{0:T(1024)(128)(4,1)S(1)} %fusion.50), kind=kOutput, calls=%fused_computation.40 | convolution fusion | flops 3239051264 | bytes 9442304 | tf_op jit(solution)/shard_map/sct,tk->skc/dot_general | solution.py:110
  27.8 0.0 copy-start.1
  27.8 2.6 copy-done.1
  30.5 2.8 fusion.64
  33.2 16.0 %reduce_window.9 = f32[6,512,256]{2,1,0:T(8,128)} reduce-window(f32[6,512,256]{2,1,0:T(8,128)} %bitcast.46, f32[]{:T(128)} %constant.167.clone.1), window={size=1x17x1 pad=0_0x8_8x0_0}, to_apply=%region_0.1 | reduce-window | flops 12582912 | bytes 6291460 | tf_op jit(solution)/shard_map/reduce_window | solution.py:58
  49.2 5.1 %divide_convert_fusion.1 = (bf16[6,32,1,16,256]{4,3,2,1,0:T(8,128)(2,1)S(1)}, bf16[6,32,1,16,256]{4,3,2,1,0:T(8,128)(2,1)S(1)}) fusion(f32[6,32,2,16,256]{4,3,2,1,0:T(8,128)} %bitcast.44, f32[6,256]{1,0:T(8,128)S(1)} %multiply_add_fusion, f32[6,32,1,16,256]{4,3,2,1,0:T(8,128)} %bitcast.45, f32[32,16]{1,0:T(8,128)S(1)} %add_convert_fusion), kind=kLoop, calls=%fused_computation.36 | loop fusion | flops 4718592 | bytes 12591104 | tf_op jit(solution)/shard_map/convert.14
  54.4 0.0 copy-start.3
  54.4 0.0 copy-start.2
  54.4 1.9 pad_maximum_fusion.1
  56.3 7.8 %collective-permute-start = (bf16[6,1024,256]{2,1,0:T(8,128)(2,1)}, bf16[6,1024,256]{2,1,0:T(8,128)(2,1)}, u32[]{:S(2)}, u32[]{:S(2)}) collective-permute-start(bf16[6,1024,256]{2,1,0:T(8,128)(2,1)} %bitcast.13), channel_id=1, source_target_pairs={{0,24},{8,32},{16,40},{24,48},{32,56},{40,64},{48,72},{56,80},{64,... | collective-permute-start | bytes 9437192 | tf_op jit(solution)/shard_map/ppermute | solution.py:21
  64.1 3.0 collective-permute-start.1
  67.1 1.9 collective-permute-start.2
  69.1 4.0 collective-permute-start.3
  73.1 1.3 collective-permute-start.4
  74.4 56.2 %collective-permute-done = bf16[6,1024,256]{2,1,0:T(8,128)(2,1)} collective-permute-done((bf16[6,1024,256]{2,1,0:T(8,128)(2,1)}, bf16[6,1024,256]{2,1,0:T(8,128)(2,1)}, u32[]{:S(2)}, u32[]{:S(2)}) %collective-permute-start) | collective-permute-done | bytes 3145760 | tf_op jit(solution)/shard_map/ppermute | solution.py:21
  130.6 1.3 collective-permute-start.5
  131.9 0.0 copy-done.3
  131.9 0.7 dynamic_slice.17
  132.6 0.0 copy-done.2
  132.6 0.2 dynamic-slice_reduce_fusion
  132.8 63.9 %collective-permute-done.1 = bf16[6,1024,256]{2,1,0:T(8,128)(2,1)} collective-permute-done((bf16[6,1024,256]{2,1,0:T(8,128)(2,1)}, bf16[6,1024,256]{2,1,0:T(8,128)(2,1)}, u32[]{:S(2)}, u32[]{:S(2)}) %collective-permute-start.1) | collective-permute-done | bytes 3145760 | tf_op jit(solution)/shard_map/ppermute | solution.py:21
  196.7 33.7 %collective-permute-done.2 = bf16[6,1024,256]{2,1,0:T(8,128)(2,1)} collective-permute-done((bf16[6,1024,256]{2,1,0:T(8,128)(2,1)}, bf16[6,1024,256]{2,1,0:T(8,128)(2,1)}, u32[]{:S(2)}, u32[]{:S(2)}) %collective-permute-start.2) | collective-permute-done | bytes 3145760 | tf_op jit(solution)/shard_map/ppermute | solution.py:21
  230.4 0.0 collective-permute-done.3
  230.4 0.0 collective-permute-done.4
  230.4 36.1 %collective-permute-done.5 = bf16[6,1024,256]{2,1,0:T(8,128)(2,1)} collective-permute-done((bf16[6,1024,256]{2,1,0:T(8,128)(2,1)}, bf16[6,1024,256]{2,1,0:T(8,128)(2,1)}, u32[]{:S(2)}, u32[]{:S(2)}) %collective-permute-start.5) | collective-permute-done | bytes 3145760 | tf_op jit(solution)/shard_map/ppermute | solution.py:21
  266.5 3.0 broadcast_in_dim.37.clone
  269.5 33.9 %while.14 = (s32[]{:T(128)}, f32[3,1024,256]{1,0,2:T(4,128)}, s32[]{:T(128)}, bf16[6,1024,256]{2,1,0:T(8,128)(2,1)}, s32[3]{0:T(128)S(1)}, /*index=5*/bf16[6,102...) while((s32[]{:T(128)}, f32[3,1024,256]{1,0,2:T(4,128)}, ...), condition=%wide.region_11.12_spmd, body=%wide.region_2.11_spmd.sunk | while | flops 9437194 | bytes 19923228 | solution.py:131
  270.1 0.7 dynamic_slice.21
  272.9 1.9 conditional.2
  272.9 1.9 copy.23
  274.8 3.3 fusion.67
  278.1 1.1 pad_maximum_fusion.3
  279.2 3.6 copy.20
  282.8 20.0 %dynamic_update_slice.11 = f32[3,1024,256]{1,0,2:T(4,128)} dynamic-update-slice(f32[3,1024,256]{1,0,2:T(4,128)} %get-tuple-element.457, f32[1,1024,256]{1,0,2:T(1,128)} %copy.20, s32[]{:T(128)S(6)} %select_n.161, s32[]{:T(128)} %constant.166.clone.1..sunk, s32[]{:T(128)} %constant.166.clone.1..sunk) | dynamic-update-slice | bytes 2097156 | tf_op jit(solution)/shard_map/while/body/jit(dynamic_update_index_in_dim)/dynamic_update_slice | solution.py:128
  303.4 0.0 copy-start.4
  303.4 0.0 all-reduce.3.cloned.1.call-update
  303.4 0.6 copy-done.4
  304.1 0.6 dynamic-slice
  305.3 177.6 %all-reduce.3.cloned.1.call-done = f32[3,1024,256]{1,0,2:T(4,128)} async-done(((f32[3,1024,256]{1,0,2:T(4,128)}), f32[3,1024,256]{1,0,2:T(4,128)}) %all-reduce.3.cloned.1.call-update) | async-done | bytes 3145744
  482.9 1.1 constant_dynamic-slice_fusion
  484.1 21.7 %fusion.39 = f32[3,32,1024]{2,1,0:T(8,128)} fusion(s32[1024]{0:T(1024)S(1)} %fusion.53, pred[1024]{0:T(1024)(128)(4,1)S(1)} %fusion.50, f32[3,1024,32]{1,0,2:T(4,128)S(1)} %constant_dynamic-slice_fusion), kind=kOutput, calls=%fused_computation.53 | convolution fusion | flops 1224835072 | bytes 791552 | tf_op jit(solution)/shard_map/pkc,kt->pct/dot_general | solution.py:135
  (4 shorter events, 0.0 us)
Async XLA Ops:
  6.5 1.9 copy-start
  6.5 476.4 %all-reduce.3.cloned.1.call-start = ((), (), s32[]{:S(2)}) async-start(), calls=%async_computation | async-start | bytes 8388608
  27.8 2.7 copy-start.1
  54.4 77.5 %copy-start.3 = (s32[32]{0:T(128)S(1)}, s32[32]{0:T(128)}, u32[]{:S(2)}) copy-start(s32[32]{0:T(128)} %param.13) | copy-start | bytes 388
  54.4 78.2 %copy-start.2 = (s32[32,3]{0,1:T(4,128)S(1)}, s32[32,3]{0,1:T(4,128)}, u32[]{:S(2)}) copy-start(s32[32,3]{0,1:T(4,128)} %param.12) | copy-start | bytes 1156
  56.3 74.3 %collective-permute-start = (bf16[6,1024,256]{2,1,0:T(8,128)(2,1)}, bf16[6,1024,256]{2,1,0:T(8,128)(2,1)}, u32[]{:S(2)}, u32[]{:S(2)}) collective-permute-start(bf16[6,1024,256]{2,1,0:T(8,128)(2,1)} %bitcast.13), channel_id=1, source_target_pairs={{0,24},{8,32},{16,40},{24,48},{32,56},{40,64},{48,72},{56,80},{64,... | collective-permute-start | bytes 9437192 | tf_op jit(solution)/shard_map/ppermute | solution.py:21
  64.1 132.5 %collective-permute-start.1 = (bf16[6,1024,256]{2,1,0:T(8,128)(2,1)}, bf16[6,1024,256]{2,1,0:T(8,128)(2,1)}, u32[]{:S(2)}, u32[]{:S(2)}) collective-permute-start(bf16[6,1024,256]{2,1,0:T(8,128)(2,1)} %bitcast.13), channel_id=1, source_target_pairs={{0,16},{8,24},{16,32},{24,40},{32,48},{40,56},{48,64},{56,72},{64,... | collective-permute-start | bytes 9437192 | tf_op jit(solution)/shard_map/ppermute | solution.py:21
  67.1 163.2 %collective-permute-start.2 = (bf16[6,1024,256]{2,1,0:T(8,128)(2,1)}, bf16[6,1024,256]{2,1,0:T(8,128)(2,1)}, u32[]{:S(2)}, u32[]{:S(2)}) collective-permute-start(bf16[6,1024,256]{2,1,0:T(8,128)(2,1)} %bitcast.13), channel_id=1, source_target_pairs={{0,8},{8,16},{16,24},{24,32},{32,40},{40,48},{48,56},{56,64},{64,7... | collective-permute-start | bytes 9437192 | tf_op jit(solution)/shard_map/ppermute | solution.py:21
  69.1 161.3 %collective-permute-start.3 = (bf16[6,1024,256]{2,1,0:T(8,128)(2,1)}, bf16[6,1024,256]{2,1,0:T(8,128)(2,1)}, u32[]{:S(2)}, u32[]{:S(2)}) collective-permute-start(bf16[6,1024,256]{2,1,0:T(8,128)(2,1)} %bitcast.13), channel_id=1, source_target_pairs={{8,0},{16,8},{24,16},{32,24},{40,32},{48,40},{56,48},{64,56},{72,6... | collective-permute-start | bytes 9437192 | tf_op jit(solution)/shard_map/ppermute | solution.py:21
  73.1 157.3 %collective-permute-start.4 = (bf16[6,1024,256]{2,1,0:T(8,128)(2,1)}, bf16[6,1024,256]{2,1,0:T(8,128)(2,1)}, u32[]{:S(2)}, u32[]{:S(2)}) collective-permute-start(bf16[6,1024,256]{2,1,0:T(8,128)(2,1)} %bitcast.13), channel_id=1, source_target_pairs={{16,0},{24,8},{32,16},{40,24},{48,32},{56,40},{64,48},{72,56},{80,... | collective-permute-start | bytes 9437192 | tf_op jit(solution)/shard_map/ppermute | solution.py:21
  130.6 135.8 %collective-permute-start.5 = (bf16[6,1024,256]{2,1,0:T(8,128)(2,1)}, bf16[6,1024,256]{2,1,0:T(8,128)(2,1)}, u32[]{:S(2)}, u32[]{:S(2)}) collective-permute-start(bf16[6,1024,256]{2,1,0:T(8,128)(2,1)} %bitcast.13), channel_id=1, source_target_pairs={{24,0},{32,8},{40,16},{48,24},{56,32},{64,40},{72,48},{80,56},{88,... | collective-permute-start | bytes 9437192 | tf_op jit(solution)/shard_map/ppermute | solution.py:21
  303.4 0.7 copy-start.4
Sparse Core Ops, SparseCore 0:
  303.5 179.3 all-reduce.2
where the time goes:
time: 515 us; the launch traced here: 513 us
  waiting for transfers between devices  368 us (71%)
  matrix products  41.1 us (8%)
  local copies, waits for them, and re-layouts  36.9 us (7%)
  other arithmetic  30.2 us (6%)
  starting transfers between devices  19.3 us (4%)
  between operations  14.2 us (3%)
    ppermute x6, waiting for transfers between devices, from_behind(): lax.ppermute(value, axis, [(source, source + steps) for source in range(f...  190 us
    unnamed x2, waiting for transfers between devices  178 us
    dynamic_update_slice x2, local copies, waits for them, and re-layouts, add_pair(): return lax.dynamic_update_index_in_dim(totals, product, slot_index, 0)  23.6 us
    dot_general x1, matrix products, body(): jnp.einsum('pkc,kt->pct', stacked, inverse, precision=lax.Precision.HIGHE...  21.7 us
    dot_general x1, matrix products, body(): jnp.einsum('sct,tk->skc', traces, dft_table, preferred_element_type=jnp.f...  19.4 us
    ppermute x6, starting transfers between devices, from_behind(): lax.ppermute(value, axis, [(source, source + steps) for source in range(f...  19.3 us
    another operation x1, other arithmetic, whiten(): lax.reduce_window(amplitude, jnp.zeros((), amplitude.dtype), lax.add, (1,...  16 us
  transfers between devices with their start and end apart: 7, of which 5 were waited for; matrix products, arithmetic and copies ran while one was open for 0% of the time, Pallas kernels for 0%

commit v1 on v0

v1 whole, which is shorter than its diff:
```python
import functools
import math

import jax
import jax.numpy as jnp
import numpy as np
from jax import lax
from jax.experimental import pallas as pl
from jax.experimental.pallas import tpu as pltpu
from jax.sharding import PartitionSpec as P

MESH = pl.DeviceIdType.MESH
RADIUS = 8
HALO = 3
SLOTS = 3
WATER = 0.8
EPS = 1e-06
ROW = 8
WIN = 8
HALF = 16
LANES = 128


def forward_table(length):
    column = np.arange(length)
    phase = np.arange(length)[:, None] * (column % (length // 2))[None, :] % length
    angles = phase * (2.0 * math.pi / length)
    table = np.where(column[None, :] < length // 2, np.cos(angles), -np.sin(angles))
    return table.astype(jnp.bfloat16)


def inverse_table(length):
    column = np.arange(length)
    phase = np.arange(length)[None, :] * (column % (length // 2))[:, None] % length
    angles = phase * (2.0 * math.pi / length)
    table = np.where(column[:, None] < length // 2, np.cos(angles), -np.sin(angles))
    return table.astype(jnp.bfloat16)


def band_table(bins):
    place = np.arange(bins)
    return (np.abs(place[:, None] - place[None, :]) <= RADIUS).astype(jnp.bfloat16)


def window_weight(bins):
    place = np.arange(bins)
    count = np.minimum(place + RADIUS, bins - 1) - np.maximum(place - RADIUS, 0) + 1
    return np.broadcast_to((1.0 / count).astype(np.float32), (8, bins))


def kernel(
    norm, offsets, counts, traces, forward, band, inverse, weight, out,
    tr, fwd, bnd, inv, spec, high, low, smooth, water, white, got, near, part, zout, zin, fout, fin, left,
    tab_sem, tr_sem, xs, xr, ys, yr, zs, zr, fs, fr,
):
    segments, bins = tr.shape[1], bnd.shape[0]
    groups = bins // LANES
    chan, win = lax.axis_index("chan"), lax.axis_index("win")
    row, place = chan // ROW, chan % ROW
    first = row * ROW
    above = lax.rem(row + 1, 4) * ROW + place
    below = lax.rem(row + 3, 4) * ROW + place
    after, before = lax.rem(win + 1, WIN), lax.rem(win + WIN - 1, WIN)

    barrier = pltpu.get_barrier_semaphore()
    mates = [(first + lax.rem(place + k, ROW), win) for k in range(1, ROW)]
    partners = mates + [(above, win), (below, win), (chan, after), (chan, before)]
    for partner in partners:
        pl.semaphore_signal(barrier, inc=1, device_id=partner, device_id_type=MESH)

    def chunk_of(t):
        half = 4 - (t + 1) // 2
        return lax.rem(win + jnp.where(t % 2 == 1, WIN - half, half), WIN)

    def trace_copy(t):
        rows = pl.ds(pl.multiple_of(chunk_of(t) * 2 * HALF, 2 * HALF), 2 * HALF)
        return pltpu.make_async_copy(traces.at[:, rows, :], tr.at[t], tr_sem.at[t])

    tables = [
        pltpu.make_async_copy(forward, fwd, tab_sem.at[0]),
        pltpu.make_async_copy(band, bnd, tab_sem.at[1]),
        pltpu.make_async_copy(inverse, inv, tab_sem.at[2]),
    ]
    tables[0].start()
    trace_copy(0).start()
    tables[1].start()

    def start_traces(t, carry):
        trace_copy(t).start()
        return carry

    lax.fori_loop(1, WIN, start_traces, 0)
    tables[2].start()
    tables[0].wait()
    tables[1].wait()

    def whiten(t):
        trace_copy(t).wait()
        lhs = tr[t].reshape(segments * 2 * HALF, 2 * bins)
        spec[...] = jnp.dot(lhs, fwd[...], preferred_element_type=jnp.float32)

        def amplitudes(i, carry):
            rows = pl.ds(pl.multiple_of(i * HALF, HALF), HALF)
            re, im = spec[rows, :bins], spec[rows, bins:]
            amp = jnp.sqrt(re * re + im * im)
            top = amp.astype(jnp.bfloat16)
            high[rows, :] = top
            low[rows, :] = (amp - top.astype(jnp.float32)).astype(jnp.bfloat16)
            mean = jnp.sum(amp, axis=1, keepdims=True) * (1.0 / bins)
            water[rows, :] = jnp.broadcast_to(WATER * mean + EPS, (HALF, LANES))
            return carry

        lax.fori_loop(0, 2 * segments, amplitudes, 0)
        smooth[...] = jnp.dot(high[...], bnd[...], preferred_element_type=jnp.float32) + jnp.dot(
            low[...], bnd[...], preferred_element_type=jnp.float32
        )

        def divide(s, carry):
            for h in range(2):
                rows = pl.ds(pl.multiple_of(s * 2 * HALF + h * HALF, HALF), HALF)
                level = water[rows, :]
                for g in range(groups):
                    lanes = slice(g * LANES, (g + 1) * LANES)
                    scale = 1.0 / jnp.maximum(smooth[rows, lanes] * weight[0:1, lanes], level)
                    re = spec[rows, lanes] * scale
                    im = spec[rows, slice(bins + g * LANES, bins + (g + 1) * LANES)] * scale
                    white[t, 2 * g + h, 0, s] = re.astype(jnp.bfloat16)
                    white[t, 2 * g + h, 1, s] = im.astype(jnp.bfloat16)
            return carry

        lax.fori_loop(0, segments, divide, 0)

    def send_row(t):
        for k, mate in enumerate(mates):
            other = lax.rem(place + k + 1, ROW)
            pltpu.make_async_remote_copy(
                white.at[t, other], got.at[t, HALO + place], xs.at[t], xr.at[t], device_id=mate, device_id_type=MESH
            ).start()
        got[t, HALO + place] = white[t, place]

    def row_wait(t):
        block = got.at[t, pl.ds(0, ROW - 1)]
        return pltpu.make_async_remote_copy(block, block, xs.at[t], xr.at[t], device_id=mates[0], device_id_type=MESH)

    def near_copy(t, source, target, device):
        return pltpu.make_async_remote_copy(
            got.at[t, pl.ds(source, HALO)],
            got.at[t, pl.ds(target, HALO)],
            ys.at[t],
            yr.at[t],
            device_id=(device, win),
            device_id_type=MESH,
        )

    def near_wait(t):
        block = got.at[t, pl.ds(0, 2 * HALO)]
        return pltpu.make_async_remote_copy(
            block, block, ys.at[t], yr.at[t], device_id=(above, win), device_id_type=MESH
        )

    def chain_copy(t):
        target = jnp.where((t % 2 == 0) & (t > 0), after, before)
        return pltpu.make_async_remote_copy(
            zout.at[t], zin.at[t], zs.at[t], zr.at[t], device_id=(chan, target), device_id_type=MESH
        )

    def cross(t):
        def move(b, carry):
            near[b] = got[t, b]
            return carry

        lax.fori_loop(0, ROW + 2 * HALO, move, 0)

        def owner(j, carry):
            source = [
                (near[HALO + j, 0, s].astype(jnp.float32), near[HALO + j, 1, s].astype(jnp.float32))
                for s in range(segments)
            ]
            for p in range(SLOTS):
                receiver = HALO + j + offsets[first + j, p]
                live = p < counts[first + j]
                total_re = jnp.zeros((HALF, LANES), jnp.float32)
                total_im = jnp.zeros((HALF, LANES), jnp.float32)
                for s, (ar, ai) in enumerate(source):
                    br = near[receiver, 0, s].astype(jnp.float32)
                    bi = near[receiver, 1, s].astype(jnp.float32)
                    total_re += ar * br + ai * bi
                    total_im += ar * bi - ai * br
                part[SLOTS * j + p, 0] = jnp.where(live, total_re, 0.0)
                part[SLOTS * j + p, 1] = jnp.where(live, total_im, 0.0)
            return carry

        lax.fori_loop(0, ROW, owner, 0)

    def add_up(t):
        @pl.when((t == 1) | (t > 2))
        def _():
            slot = jnp.where(t == 1, 0, jnp.maximum(t - 2, 0))
            chain_copy(slot).wait_recv()

            def add(q, carry):
                part[q] = part[q] + zin[slot, q].astype(jnp.float32)
                return carry

            lax.fori_loop(0, SLOTS * ROW, add, 0)

        @pl.when(t < WIN - 1)
        def _():
            def store(q, carry):
                zout[t, q] = part[q].astype(jnp.bfloat16)
                return carry

            lax.fori_loop(0, SLOTS * ROW, store, 0)
            chain_copy(t).start()

    def forward_step(t, carry):
        whiten(t)

        @pl.when(t == 0)
        def _():
            pl.semaphore_wait(barrier, len(partners))

        send_row(t)
        return carry

    lax.fori_loop(0, WIN, forward_step, 0)

    def pair_step(t, carry):
        @pl.when(t < WIN)
        def _():
            row_wait(t).wait_recv()
            near_copy(t, HALO, HALO + ROW, below).start()
            near_copy(t, ROW, 0, above).start()

        @pl.when(t > 0)
        def _():
            near_wait(t - 1).wait_recv()
            cross(t - 1)
            add_up(t - 1)

        return carry

    lax.fori_loop(0, WIN + 1, pair_step, 0)

    last = WIN - 2
    chain_copy(last).wait_recv()

    def finish(q, carry):
        fout[q] = (part[q] + zin[last, q].astype(jnp.float32)).astype(jnp.bfloat16)
        return carry

    lax.fori_loop(0, SLOTS * ROW, finish, 0)
    for k, mate in enumerate(mates):
        other = lax.rem(place + k + 1, ROW)
        pltpu.make_async_remote_copy(
            fout.at[pl.ds(SLOTS * other, SLOTS)], fin.at[place], fs, fr, device_id=mate, device_id_type=MESH
        ).start()
    fin[place] = fout[pl.ds(SLOTS * place, SLOTS)]
    tables[2].wait()
    final = fin.at[pl.ds(0, ROW - 1)]
    final_wait = pltpu.make_async_remote_copy(final, final, fs, fr, device_id=mates[0], device_id_type=MESH)
    final_wait.wait_recv()
    for g in range(groups):
        for h in range(2):
            for p in range(SLOTS):
                rows = slice((2 * p + h) * HALF, (2 * p + h + 1) * HALF)
                left[rows, g * LANES : (g + 1) * LANES] = fin[2 * g + h, p, 0]
                left[rows, bins + g * LANES : bins + (g + 1) * LANES] = fin[2 * g + h, p, 1]
    result = jnp.dot(left[...], inv[...], preferred_element_type=jnp.float32) * norm
    out[...] = result.reshape(out.shape)

    final_wait.wait_send()

    def drain(t, carry):
        row_wait(t).wait_send()
        near_wait(t).wait_send()

        @pl.when(t < WIN - 1)
        def _():
            chain_copy(t).wait_send()

        return carry

    lax.fori_loop(0, WIN, drain, 0)


def body(traces, offsets, counts):
    segments, channels, length = traces.shape
    bins = length // 2
    norm = 1.0 / math.sqrt(bins * segments * WIN)
    rows = segments * 2 * HALF
    bf16, f32 = jnp.bfloat16, jnp.float32
    pairs = SLOTS * ROW
    share = (2, HALF, LANES)
    block = (2, segments, HALF, LANES)
    any_space, vmem, smem = (pl.BlockSpec(memory_space=s) for s in (pl.ANY, pltpu.VMEM, pltpu.SMEM))
    dma = pltpu.SemaphoreType.DMA
    return pl.pallas_call(
        functools.partial(kernel, norm),
        out_shape=jax.ShapeDtypeStruct((SLOTS, channels // WIN, length), f32),
        in_specs=[smem, smem, any_space, any_space, any_space, any_space, vmem],
        out_specs=vmem,
        scratch_shapes=[
            pltpu.VMEM((WIN, segments, 2 * HALF, length), bf16),
            pltpu.VMEM((length, length), bf16),
            pltpu.VMEM((bins, bins), bf16),
            pltpu.VMEM((length, length), bf16),
            pltpu.VMEM((rows, length), f32),
            pltpu.VMEM((rows, bins), bf16),
            pltpu.VMEM((rows, bins), bf16),
            pltpu.VMEM((rows, bins), f32),
            pltpu.VMEM((rows, LANES), f32),
            pltpu.VMEM((WIN, ROW) + block, bf16),
            pltpu.VMEM((WIN, ROW + 2 * HALO) + block, bf16),
            pltpu.VMEM((ROW + 2 * HALO,) + block, bf16),
            pltpu.VMEM((pairs,) + share, f32),
            pltpu.VMEM((WIN - 1, pairs) + share, bf16),
            pltpu.VMEM((WIN - 1, pairs) + share, bf16),
            pltpu.VMEM((pairs,) + share, bf16),
            pltpu.VMEM((ROW, SLOTS) + share, bf16),
            pltpu.VMEM((SLOTS * 2 * HALF, length), bf16),
            dma((3,)),
            dma((WIN,)),
            dma((WIN,)),
            dma((WIN,)),
            dma((WIN,)),
            dma((WIN,)),
            dma((WIN - 1,)),
            dma((WIN - 1,)),
            dma,
            dma,
        ],
        compiler_params=pltpu.CompilerParams(collective_id=0, has_side_effects=True, vmem_limit_bytes=48 << 20),
    )(
        offsets,
        counts,
        traces,
        jnp.asarray(forward_table(length)),
        jnp.asarray(band_table(bins)),
        jnp.asarray(inverse_table(length)),
        jnp.asarray(window_weight(bins)),
    )


def solution(mesh):
    in_specs = (P("win", "chan", None), P(), P())
    out_specs = P("chan", "win", None)
    return jax.shard_map(body, mesh=mesh, in_specs=in_specs, out_specs=out_specs, check_vma=False)
```

time: 515 us -> 74.1 us (0.14)
  waiting for transfers between devices: 368 us -> 0 us
  Pallas kernels: 0 us -> 66.7 us
  matrix products: 41.1 us -> 0 us
  other arithmetic: 30.2 us -> 0 us
  local copies, waits for them, and re-layouts: 36.9 us -> 7.07 us
  starting transfers between devices: 19.3 us -> 0 us
  between operations: 14.2 us -> 0.01 us
    ppermute x6 -> x0, waiting for transfers between devices: 190 us -> none  [from_behind(): lax.ppermute(value, axis, [(source, source + steps) for source in range(f...]
    unnamed x2 -> x0, waiting for transfers between devices: 178 us -> none
    pallas_call x0 -> x1, Pallas kernels: none -> 66.7 us  [body(): pl.pallas_call(functools.partial(kernel, norm), out_shape=jax.ShapeDtypeS...]
    dot_general x2 -> x0, matrix products: 41.1 us -> none  [the longest x1 21.7 us: body(): jnp.einsum('pkc,kt->pct', stacked, inverse, precision=lax.Precision.HIGHE...]
    another operation x4 -> x0, other arithmetic: 24.1 us -> none  [the longest x1 16 us: whiten(): lax.reduce_window(amplitude, jnp.zeros((), amplitude.dtype), lax.add, (1,...]
    dynamic_update_slice x2 -> x0, local copies, waits for them, and re-layouts: 23.6 us -> none  [add_pair(): return lax.dynamic_update_index_in_dim(totals, product, slot_index, 0)]
    ppermute x6 -> x0, starting transfers between devices: 19.3 us -> none  [from_behind(): lax.ppermute(value, axis, [(source, source + steps) for source in range(f...]
    reduce_sum x2 -> x0, other arithmetic: 6.02 us -> none  [the longest x1 3.26 us: cross_terms(): jnp.sum(source_real * receiver_real + source_imag * receiver_imag, axis=s...]
  transfers between devices with their start and end apart: 7 -> 0, of which waited for: 5 -> 0; matrix products, arithmetic and copies ran while one was open for 0% -> 0% of each run, Pallas kernels for 0% -> 0%
where the time goes in v1:
time: 74.1 us; the launch traced here: 73.8 us
  Pallas kernels  66.7 us (90%)
  local copies, waits for them, and re-layouts  7.07 us (10%)
    pallas_call x1, Pallas kernels, body(): pl.pallas_call(functools.partial(kernel, norm), out_shape=jax.ShapeDtypeS...  66.7 us
    unnamed x10, local copies, waits for them, and re-layouts  6.39 us

profile of v1, /device:TPU:1, one launch (start us, length us, event | category | flops | bytes accessed | tf_op | source)
XLA Modules:
  0.0 73.8 jit_solution(11927697561911859014)
XLA Ops:
  0.0 0.8 %copy.8.offsets = s32[32,3]{1,0:T(8,128)S(1)} copy(s32[32,3]{0,1:T(4,128)} %param.8) | data formatting | bytes 768 | tf_op args[1]
  0.8 0.7 jit_solution_.3.weight
  1.4 0.0 copy-start
  1.4 1.6 %copy-done = bf16[1024,1024]{1,0:T(8,128)(2,1)S(1)} copy-done((bf16[1024,1024]{1,0:T(8,128)(2,1)S(1)}, bf16[1024,1024]{1,0:T(8,128)(2,1)}, u32[]{:S(2)}) %copy-start) | copy-done | bytes 2097176
  3.0 0.0 copy-start.1
  3.0 1.6 %copy-done.1 = bf16[1024,1024]{1,0:T(8,128)(2,1)S(1)} copy-done((bf16[1024,1024]{1,0:T(8,128)(2,1)S(1)}, bf16[1024,1024]{1,0:T(8,128)(2,1)}, u32[]{:S(2)}) %copy-start.1) | copy-done | bytes 2097176
  4.6 0.0 copy-start.2
  4.6 1.0 %copy-done.2 = bf16[512,512]{1,0:T(8,128)(2,1)S(1)} copy-done((bf16[512,512]{1,0:T(8,128)(2,1)S(1)}, bf16[512,512]{1,0:T(8,128)(2,1)}, u32[]{:S(2)}) %copy-start.2) | copy-done | bytes 524312
  5.7 0.0 copy-start.3
  5.7 0.7 copy-done.3
  6.3 66.7 %shard_map.73 = f32[3,32,1024]{2,1,0:T(8,128)S(1)} custom-call(s32[32,3]{1,0:T(8,128)S(1)} %copy.8.offsets, s32[32]{0:T(128)S(1)} %copy-done.3, bf16[6,256,1024]{2,1,0:T(8,128)(2,1)} %traces.1, bf16[1024,1024]{1,0:T(8,128)(2,1)S(1)} %copy-done.1, bf16[512,512]{1,0:T(8,128)(2,1)S(1)} %copy-done.2, bf16[1024,1024]{1,0:T(8,128)(2,1)S(1)} %copy-done, ...), custom_call_target="tpu_custom_call" | custom-call | tf_op jit(solution)/shard_map/pallas_call | solution.py:298
  73.1 0.7 %copy.10 = f32[3,32,1024]{2,1,0:T(8,128)} copy(f32[3,32,1024]{2,1,0:T(8,128)S(1)} %shard_map.73) | data formatting | bytes 786432
Async XLA Ops:
  1.4 1.6 %copy-start = (bf16[1024,1024]{1,0:T(8,128)(2,1)S(1)}, bf16[1024,1024]{1,0:T(8,128)(2,1)}, u32[]{:S(2)}) copy-start(bf16[1024,1024]{1,0:T(8,128)(2,1)} %constant.10.clone.inverse) | copy-start | bytes 6291460
  3.0 1.6 %copy-start.1 = (bf16[1024,1024]{1,0:T(8,128)(2,1)S(1)}, bf16[1024,1024]{1,0:T(8,128)(2,1)}, u32[]{:S(2)}) copy-start(bf16[1024,1024]{1,0:T(8,128)(2,1)} %constant.8.clone.forward) | copy-start | bytes 6291460
  4.6 1.0 %copy-start.2 = (bf16[512,512]{1,0:T(8,128)(2,1)S(1)}, bf16[512,512]{1,0:T(8,128)(2,1)}, u32[]{:S(2)}) copy-start(bf16[512,512]{1,0:T(8,128)(2,1)} %constant.9.clone.band) | copy-start | bytes 1572868
  5.7 0.7 copy-start.3

commit v2 on v1

v2 whole, which is shorter than its diff:
```python
import functools
import math

import jax
import jax.numpy as jnp
import numpy as np
from jax import lax
from jax.experimental import pallas as pl
from jax.experimental.pallas import tpu as pltpu
from jax.sharding import PartitionSpec as P

MESH = pl.DeviceIdType.MESH
RADIUS = 8
HALO = 3
SLOTS = 3
WATER = 0.8
EPS = 1e-06
ROW = 8
WIN = 8
PART = 16
SHARE = 8
LANES = 128
VMEM_BYTES = 62 << 20

ORDER = [(-4, 0), (-4, 1), (-3, 0), (-3, 1), (3, 0), (3, 1), (-2, 0), (-2, 1), (2, 0), (2, 1)]
ORDER += [(-1, 0), (1, 0), (-1, 1), (1, 1), (0, 0), (0, 1)]
STEPS = len(ORDER)
OUTSIDE = STEPS - 2
AHEAD = 3
BEHIND = 5


def forward_table(length):
    column = np.arange(length)
    phase = np.arange(length)[:, None] * (column % (length // 2))[None, :] % length
    angles = phase * (2.0 * math.pi / length)
    table = np.where(column[None, :] < length // 2, np.cos(angles), -np.sin(angles))
    return table.astype(jnp.bfloat16)


def inverse_table(length):
    column = np.arange(length)
    phase = np.arange(length)[None, :] * (column % (length // 2))[:, None] % length
    angles = phase * (2.0 * math.pi / length)
    table = np.where(column[:, None] < length // 2, np.cos(angles), -np.sin(angles))
    return table.astype(jnp.bfloat16)


def band_table(bins):
    place = np.arange(bins)
    return (np.abs(place[:, None] - place[None, :]) <= RADIUS).astype(jnp.bfloat16)


def arrival(step):
    where, half = ORDER[step]
    if where in (-4, 3):
        return -1
    return ORDER.index((where - 1 if where <= 0 else where + 1, half))


def look_up(step, values):
    found = jnp.int32(values[0])
    for k, value in enumerate(values[1:], 1):
        if value != values[0]:
            found = jnp.where(step == k, jnp.int32(value), found)
    return found


def kernel(
    norm, offsets_in, counts_in, traces, forward, band, inverse, out,
    offsets, counts, tr, fwd, bnd, inv, weight, spec, high, low, smooth, water, white, got, near, part, zout, zin,
    fout, fin, left, tab_sem, tr_sem, xs, xr, ys, yr, zs, zr, fs, fr,
):
    segments, bins = tr.shape[1], bnd.shape[0]
    groups = bins // LANES
    chan, win = lax.axis_index("chan"), lax.axis_index("win")
    row, place = chan // ROW, chan % ROW
    first = row * ROW
    above = lax.rem(row + 1, 4) * ROW + place
    below = lax.rem(row + 3, 4) * ROW + place
    after, before = lax.rem(win + 1, WIN), lax.rem(win + WIN - 1, WIN)

    barrier = pltpu.get_barrier_semaphore()
    mates = [(first + lax.rem(place + k, ROW), win) for k in range(1, ROW)]
    partners = mates + [(above, win), (below, win), (chan, after), (chan, before)]
    for partner in partners:
        pl.semaphore_signal(barrier, inc=1, device_id=partner, device_id_type=MESH)

    def trace_copy(i):
        target = lax.rem(win + look_up(i, [(where + WIN) % WIN for where, _ in ORDER]), WIN)
        half = look_up(i, [half for _, half in ORDER])
        rows = pl.ds(pl.multiple_of((2 * target + half) * PART, PART), PART)
        return pltpu.make_async_copy(traces.at[:, rows, :], tr.at[i], tr_sem.at[i])

    tables = [
        pltpu.make_async_copy(source, target, tab_sem.at[k])
        for k, (source, target) in enumerate(
            [(forward, fwd), (band, bnd), (inverse, inv), (offsets_in, offsets), (counts_in, counts)]
        )
    ]
    tables[0].start()
    trace_copy(0).start()
    tables[1].start()

    def start_traces(i, carry):
        trace_copy(i).start()
        return carry

    lax.fori_loop(1, STEPS, start_traces, 0)
    for table in tables[2:]:
        table.start()
    bin_of = lax.broadcasted_iota(jnp.int32, weight.shape, 1)
    count = jnp.minimum(bin_of + RADIUS, bins - 1) - jnp.maximum(bin_of - RADIUS, 0) + 1
    weight[...] = 1.0 / count.astype(jnp.float32)
    tables[0].wait()
    tables[1].wait()

    def whiten(i):
        trace_copy(i).wait()
        lhs = tr[i].reshape(segments * PART, 2 * bins)
        spec[...] = jnp.dot(lhs, fwd[...], preferred_element_type=jnp.float32)
        for s in range(segments):
            rows = slice(s * PART, (s + 1) * PART)
            re, im = spec[rows, :bins], spec[rows, bins:]
            amp = jnp.sqrt(re * re + im * im)
            top = amp.astype(jnp.bfloat16)
            high[rows, :] = top
            low[rows, :] = (amp - top.astype(jnp.float32)).astype(jnp.bfloat16)
            mean = jnp.sum(amp, axis=1, keepdims=True) * (1.0 / bins)
            water[rows, :] = jnp.broadcast_to(WATER * mean + EPS, (PART, LANES))
        smooth[...] = jnp.dot(high[...], bnd[...], preferred_element_type=jnp.float32) + jnp.dot(
            low[...], bnd[...], preferred_element_type=jnp.float32
        )
        for s in range(segments):
            rows = slice(s * PART, (s + 1) * PART)
            level = water[rows, :]
            for g in range(groups):
                lanes = slice(g * LANES, (g + 1) * LANES)
                scale = 1.0 / jnp.maximum(smooth[rows, lanes] * weight[0:1, lanes], level)
                re = spec[rows, lanes] * scale
                im = spec[rows, slice(bins + g * LANES, bins + (g + 1) * LANES)] * scale
                for h in range(2):
                    share = slice(h * SHARE, (h + 1) * SHARE)
                    both = jnp.concatenate([re[share], im[share]], axis=0)
                    white[i, 2 * g + h, s] = both.astype(jnp.bfloat16)

    def send_row(i):
        for k, mate in enumerate(mates):
            other = lax.rem(place + k + 1, ROW)
            pltpu.make_async_remote_copy(
                white.at[i, other], got.at[i, HALO + place], xs.at[i], xr.at[i], device_id=mate, device_id_type=MESH
            ).start()
        got[i, HALO + place] = white[i, place]

    def row_wait(i):
        block = got.at[i, pl.ds(0, ROW - 1)]
        return pltpu.make_async_remote_copy(block, block, xs.at[i], xr.at[i], device_id=mates[0], device_id_type=MESH)

    def near_copy(i, source, target, device):
        return pltpu.make_async_remote_copy(
            got.at[i, pl.ds(source, HALO)],
            got.at[i, pl.ds(target, HALO)],
            ys.at[i],
            yr.at[i],
            device_id=(device, win),
            device_id_type=MESH,
        )

    def near_wait(i):
        block = got.at[i, pl.ds(0, 2 * HALO)]
        return pltpu.make_async_remote_copy(
            block, block, ys.at[i], yr.at[i], device_id=(above, win), device_id_type=MESH
        )

    def chain_copy(i):
        forth = look_up(i, [int(where > 0) for where, _ in ORDER])
        target = jnp.where(forth == 1, after, before)
        return pltpu.make_async_remote_copy(
            zout.at[i], zin.at[i], zs.at[i], zr.at[i], device_id=(chan, target), device_id_type=MESH
        )

    def cross(i):
        def move(b, carry):
            near[b] = got[i, b]
            return carry

        lax.fori_loop(0, ROW + 2 * HALO, move, 0, unroll=True)

        def owner(j, carry):
            source = [near[HALO + j, s].astype(jnp.float32) for s in range(segments)]
            for p in range(SLOTS):
                receiver = HALO + j + offsets[p, first + j]
                live = p < counts[first + j]
                total_re = jnp.zeros((SHARE, LANES), jnp.float32)
                total_im = jnp.zeros((SHARE, LANES), jnp.float32)
                for s, both in enumerate(source):
                    ar, ai = both[:SHARE], both[SHARE:]
                    other = near[receiver, s].astype(jnp.float32)
                    br, bi = other[:SHARE], other[SHARE:]
                    total_re += ar * br + ai * bi
                    total_im += ar * bi - ai * br
                total = jnp.concatenate([total_re, total_im], axis=0)
                part[SLOTS * j + p] = jnp.where(live, total, 0.0)
            return carry

        lax.fori_loop(0, ROW, owner, 0, unroll=2)

    def add_up(i):
        slot = look_up(i, [max(arrival(step), 0) for step in range(STEPS)])
        joins = look_up(i, [int(arrival(step) >= 0) for step in range(STEPS)]) == 1

        @pl.when(jnp.logical_not(joins))
        def _():
            zout[i] = part[...].astype(jnp.bfloat16)
            chain_copy(i).start()

        @pl.when(joins & (i < OUTSIDE))
        def _():
            chain_copy(slot).wait_recv()
            zout[i] = (part[...] + zin[slot].astype(jnp.float32)).astype(jnp.bfloat16)
            chain_copy(i).start()

        @pl.when(i >= OUTSIDE)
        def _():
            half = i - OUTSIDE
            chain_copy(slot).wait_recv()
            chain_copy(slot + 1).wait_recv()
            total = part[...] + zin[slot].astype(jnp.float32) + zin[slot + 1].astype(jnp.float32)
            fout[half] = total.astype(jnp.bfloat16)
            for k, mate in enumerate(mates):
                other = lax.rem(place + k + 1, ROW)
                pltpu.make_async_remote_copy(
                    fout.at[half, pl.ds(SLOTS * other, SLOTS)],
                    fin.at[half, place],
                    fs.at[half],
                    fr.at[half],
                    device_id=mate,
                    device_id_type=MESH,
                ).start()
            fin[half, place] = fout[half, pl.ds(SLOTS * place, SLOTS)]

    def final_wait(half):
        block = fin.at[half, pl.ds(0, ROW - 1)]
        return pltpu.make_async_remote_copy(
            block, block, fs.at[half], fr.at[half], device_id=mates[0], device_id_type=MESH
        )

    def step(i, carry):
        @pl.when(i < STEPS)
        def _():
            whiten(i)

            @pl.when(i == 0)
            def _():
                pl.semaphore_wait(barrier, len(partners))

            send_row(i)

        @pl.when(i == BEHIND)
        def _():
            tables[3].wait()
            tables[4].wait()

        @pl.when(i >= BEHIND)
        def _():
            near_wait(i - BEHIND).wait_recv()
            cross(i - BEHIND)
            add_up(i - BEHIND)

        @pl.when((i >= AHEAD) & (i < STEPS + AHEAD))
        def _():
            row_wait(i - AHEAD).wait_recv()
            near_copy(i - AHEAD, HALO, HALO + ROW, below).start()
            near_copy(i - AHEAD, ROW, 0, above).start()

        return carry

    lax.fori_loop(0, STEPS + BEHIND, step, 0)

    tables[2].wait()
    for half in range(2):
        final_wait(half).wait_recv()
        for g in range(groups):
            for p in range(SLOTS):
                pieces = [fin[half, 2 * g + h, p].astype(jnp.float32) for h in range(2)]
                re = jnp.concatenate([piece[:SHARE] for piece in pieces], axis=0)
                im = jnp.concatenate([piece[SHARE:] for piece in pieces], axis=0)
                rows = slice(p * PART, (p + 1) * PART)
                left[rows, g * LANES : (g + 1) * LANES] = re.astype(jnp.bfloat16)
                left[rows, bins + g * LANES : bins + (g + 1) * LANES] = im.astype(jnp.bfloat16)
        result = jnp.dot(left[...], inv[...], preferred_element_type=jnp.float32) * norm
        for p in range(SLOTS):
            out[p, half * PART : (half + 1) * PART, :] = result[p * PART : (p + 1) * PART]

    for half in range(2):
        final_wait(half).wait_send()

    def drain(i, carry):
        row_wait(i).wait_send()
        near_wait(i).wait_send()

        @pl.when(i < OUTSIDE)
        def _():
            chain_copy(i).wait_send()

        return carry

    lax.fori_loop(0, STEPS, drain, 0)


def body(traces, offsets, counts):
    segments, channels, length = traces.shape
    bins = length // 2
    norm = 1.0 / math.sqrt(bins * segments * WIN)
    rows = segments * PART
    bf16, f32 = jnp.bfloat16, jnp.float32
    pairs = SLOTS * ROW
    tile = (2 * SHARE, LANES)
    block = (segments,) + tile
    any_space, vmem = pl.BlockSpec(memory_space=pl.ANY), pl.BlockSpec(memory_space=pltpu.VMEM)
    dma = pltpu.SemaphoreType.DMA
    return pl.pallas_call(
        functools.partial(kernel, norm),
        out_shape=jax.ShapeDtypeStruct((SLOTS, channels // WIN, length), f32),
        in_specs=[any_space] * 6,
        out_specs=vmem,
        scratch_shapes=[
            pltpu.SMEM(offsets.shape[::-1], jnp.int32),
            pltpu.SMEM(counts.shape, jnp.int32),
            pltpu.VMEM((STEPS, segments, PART, length), bf16),
            pltpu.VMEM((length, length), bf16),
            pltpu.VMEM((bins, bins), bf16),
            pltpu.VMEM((length, length), bf16),
            pltpu.VMEM((8, bins), f32),
            pltpu.VMEM((rows, length), f32),
            pltpu.VMEM((rows, bins), bf16),
            pltpu.VMEM((rows, bins), bf16),
            pltpu.VMEM((rows, bins), f32),
            pltpu.VMEM((rows, LANES), f32),
            pltpu.VMEM((STEPS, ROW) + block, bf16),
            pltpu.VMEM((STEPS, ROW + 2 * HALO) + block, bf16),
            pltpu.VMEM((ROW + 2 * HALO,) + block, bf16),
            pltpu.VMEM((pairs,) + tile, f32),
            pltpu.VMEM((OUTSIDE, pairs) + tile, bf16),
            pltpu.VMEM((OUTSIDE, pairs) + tile, bf16),
            pltpu.VMEM((2, pairs) + tile, bf16),
            pltpu.VMEM((2, ROW, SLOTS) + tile, bf16),
            pltpu.VMEM((SLOTS * PART, length), bf16),
            dma((5,)),
            dma((STEPS,)),
            dma((STEPS,)),
            dma((STEPS,)),
            dma((STEPS,)),
            dma((STEPS,)),
            dma((OUTSIDE,)),
            dma((OUTSIDE,)),
            dma((2,)),
            dma((2,)),
        ],
        compiler_params=pltpu.CompilerParams(collective_id=0, has_side_effects=True, vmem_limit_bytes=VMEM_BYTES),
    )(
        offsets.T,
        counts,
        traces,
        jnp.asarray(forward_table(length)),
        jnp.asarray(band_table(bins)),
        jnp.asarray(inverse_table(length)),
    )


def solution(mesh):
    in_specs = (P("win", "chan", None), P(), P())
    out_specs = P("chan", "win", None)
    return jax.shard_map(body, mesh=mesh, in_specs=in_specs, out_specs=out_specs, check_vma=False)
```

time: 74.1 us -> 61.6 us (0.83)
  Pallas kernels: 66.7 us -> 59.7 us
  local copies, waits for them, and re-layouts: 7.07 us -> 1.77 us
    pallas_call x1, Pallas kernels: 66.7 us -> 59.7 us  [body(): pl.pallas_call(functools.partial(kernel, norm), out_shape=jax.ShapeDtypeS...]
    unnamed x10 -> x1, local copies, waits for them, and re-layouts: 6.39 us -> 1.77 us
where the time goes in v2:
time: 61.6 us; the launch traced here: 61.5 us
  Pallas kernels  59.7 us (97%)
  local copies, waits for them, and re-layouts  1.77 us (3%)
    pallas_call x1, Pallas kernels, body(): pl.pallas_call(functools.partial(kernel, norm), out_shape=jax.ShapeDtypeS...  59.7 us
    unnamed x1, local copies, waits for them, and re-layouts  1.77 us

profile of v2, /device:TPU:1, one launch (start us, length us, event | category | flops | bytes accessed | tf_op | source)
XLA Modules:
  0.0 61.5 jit_solution(14000495069929242081)
XLA Ops:
  0.0 59.7 %shard_map.64 = f32[3,32,1024]{2,1,0:T(8,128)} custom-call(s32[3,32]{1,0:T(4,128)} %bitcast.1, s32[32]{0:T(128)} %counts_in.1, bf16[6,256,1024]{2,1,0:T(8,128)(2,1)} %traces.1, bf16[1024,1024]{1,0:T(8,128)(2,1)} %constant.6.clone.forward, bf16[512,512]{1,0:T(8,128)(2,1)} %constant.7.clone.band, bf16[1024,1024]{1,0:T(8,128)(2,1)} %constant.8.clone.inverse), custom_call_target="tpu_custom_call" | custom-call | tf_op jit(solution)/shard_map/pallas_call | solution.py:322
  59.7 1.8 %copy.8 = f32[3,32,1024]{2,1,0:T(8,128)} copy(f32[3,32,1024]{2,1,0:T(8,128)} %shard_map.64) | data formatting | bytes 786432

commit v3 on v2

--- a/solution.py
+++ b/solution.py
@@ -26,8 +26,8 @@
 ORDER += [(-1, 0), (1, 0), (-1, 1), (1, 1), (0, 0), (0, 1)]
 STEPS = len(ORDER)
 OUTSIDE = STEPS - 2
-AHEAD = 3
-BEHIND = 5
+WINDOW = 3
+LAG = 2
 
 
 def forward_table(length):
@@ -56,6 +56,14 @@
     if where in (-4, 3):
         return -1
     return ORDER.index((where - 1 if where <= 0 else where + 1, half))
+
+
+def toward_first(step, win):
+    lower, upper = list(range(STEPS)), list(range(STEPS))
+    lower[OUTSIDE - 4 : OUTSIDE] = [ORDER.index(entry) for entry in [(-1, 0), (-1, 1), (1, 0), (1, 1)]]
+    upper[OUTSIDE - 4 : OUTSIDE] = [ORDER.index(entry) for entry in [(1, 0), (1, 1), (-1, 0), (-1, 1)]]
+    place = jnp.where((win > 0) & (win < WIN // 2), look_up(step, lower), step)
+    return jnp.where(win > WIN // 2, look_up(step, upper), place)
 
 
 def look_up(step, values):
@@ -82,13 +90,16 @@
 
     barrier = pltpu.get_barrier_semaphore()
     mates = [(first + lax.rem(place + k, ROW), win) for k in range(1, ROW)]
-    partners = mates + [(above, win), (below, win), (chan, after), (chan, before)]
+    partners = mates + [(above, win), (below, win)]
+    beside = [(chan, after), (chan, before)]
+    odd = win % 2 == 1
     for partner in partners:
         pl.semaphore_signal(barrier, inc=1, device_id=partner, device_id_type=MESH)
 
     def trace_copy(i):
-        target = lax.rem(win + look_up(i, [(where + WIN) % WIN for where, _ in ORDER]), WIN)
-        half = look_up(i, [half for _, half in ORDER])
+        entry = toward_first(i, win)
+        target = lax.rem(win + look_up(entry, [(where + WIN) % WIN for where, _ in ORDER]), WIN)
+        half = look_up(entry, [half for _, half in ORDER])
         rows = pl.ds(pl.multiple_of((2 * target + half) * PART, PART), PART)
         return pltpu.make_async_copy(traces.at[:, rows, :], tr.at[i], tr_sem.at[i])
 
@@ -245,37 +256,50 @@
             block, block, fs.at[half], fr.at[half], device_id=mates[0], device_id_type=MESH
         )
 
-    def step(i, carry):
-        @pl.when(i < STEPS)
-        def _():
-            whiten(i)
-
-            @pl.when(i == 0)
-            def _():
-                pl.semaphore_wait(barrier, len(partners))
-
-            send_row(i)
-
-        @pl.when(i == BEHIND)
+    def step(n, carry):
+        send, arrived, paired = n - 1, n - 1 - WINDOW, n - 1 - WINDOW - LAG
+
+        @pl.when((arrived >= 0) & (arrived < STEPS))
+        def _():
+            row_wait(arrived).wait_recv()
+
+        @pl.when(send == 0)
+        def _():
+            pl.semaphore_wait(barrier, len(partners) + jnp.where(odd, len(beside), 0))
+            for partner in beside:
+                pl.semaphore_signal(barrier, inc=1, device_id=partner, device_id_type=MESH)
+
+        @pl.when((send >= 0) & (send < STEPS))
+        def _():
+            send_row(send)
+
+        @pl.when((arrived >= 0) & (arrived < STEPS))
+        def _():
+            near_copy(arrived, HALO, HALO + ROW, below).start()
+            near_copy(arrived, ROW, 0, above).start()
+
+        @pl.when(n < STEPS)
+        def _():
+            whiten(n)
+
+        @pl.when(paired == 0)
         def _():
             tables[3].wait()
             tables[4].wait()
 
-        @pl.when(i >= BEHIND)
-        def _():
-            near_wait(i - BEHIND).wait_recv()
-            cross(i - BEHIND)
-            add_up(i - BEHIND)
-
-        @pl.when((i >= AHEAD) & (i < STEPS + AHEAD))
-        def _():
-            row_wait(i - AHEAD).wait_recv()
-            near_copy(i - AHEAD, HALO, HALO + ROW, below).start()
-            near_copy(i - AHEAD, ROW, 0, above).start()
+            @pl.when(jnp.logical_not(odd))
+            def _():
+                pl.semaphore_wait(barrier, len(beside))
+
+        @pl.when(paired >= 0)
+        def _():
+            near_wait(paired).wait_recv()
+            cross(paired)
+            add_up(toward_first(paired, win))
 
         return carry
 
-    lax.fori_loop(0, STEPS + BEHIND, step, 0)
+    lax.fori_loop(0, STEPS + 1 + WINDOW + LAG, step, 0)
 
     tables[2].wait()
     for half in range(2):

time: 61.6 us -> 57.4 us (0.932)
  Pallas kernels: 59.7 us -> 55.5 us
    pallas_call x1, Pallas kernels: 59.7 us -> 55.5 us  [body(): pl.pallas_call(functools.partial(kernel, norm), out_shape=jax.ShapeDtypeS...]
where the time goes in v3:
time: 57.4 us; the launch traced here: 57.3 us
  Pallas kernels  55.5 us (97%)
  local copies, waits for them, and re-layouts  1.77 us (3%)
    pallas_call x1, Pallas kernels, body(): pl.pallas_call(functools.partial(kernel, norm), out_shape=jax.ShapeDtypeS...  55.5 us
    unnamed x1, local copies, waits for them, and re-layouts  1.77 us

profile of v3, /device:TPU:1, one launch (start us, length us, event | category | flops | bytes accessed | tf_op | source)
XLA Modules:
  0.0 57.3 jit_solution(7523735495941128691)
XLA Ops:
  0.0 55.5 %shard_map.64 = f32[3,32,1024]{2,1,0:T(8,128)} custom-call(s32[3,32]{1,0:T(4,128)} %bitcast.1, s32[32]{0:T(128)} %counts_in.1, bf16[6,256,1024]{2,1,0:T(8,128)(2,1)} %traces.1, bf16[1024,1024]{1,0:T(8,128)(2,1)} %constant.6.clone.forward, bf16[512,512]{1,0:T(8,128)(2,1)} %constant.7.clone.band, bf16[1024,1024]{1,0:T(8,128)(2,1)} %constant.8.clone.inverse), custom_call_target="tpu_custom_call" | custom-call | tf_op jit(solution)/shard_map/pallas_call | solution.py:346
  55.6 1.8 %copy.8 = f32[3,32,1024]{2,1,0:T(8,128)} copy(f32[3,32,1024]{2,1,0:T(8,128)} %shard_map.64) | data formatting | bytes 786432

commit v4 on v3

--- a/solution.py
+++ b/solution.py
@@ -22,10 +22,11 @@
 LANES = 128
 VMEM_BYTES = 62 << 20
 
-ORDER = [(-4, 0), (-4, 1), (-3, 0), (-3, 1), (3, 0), (3, 1), (-2, 0), (-2, 1), (2, 0), (2, 1)]
-ORDER += [(-1, 0), (1, 0), (-1, 1), (1, 1), (0, 0), (0, 1)]
+ORDER = [(where, half) for where in (-4, 3, -3, 2, -2, 1, -1, 0) for half in (0, 1)]
 STEPS = len(ORDER)
 OUTSIDE = STEPS - 2
+GREETED = [0, 1, 2, 0, 2, 0, 2, 1]
+CUTS = 2
 WINDOW = 3
 LAG = 2
 
@@ -58,12 +59,12 @@
     return ORDER.index((where - 1 if where <= 0 else where + 1, half))
 
 
-def toward_first(step, win):
-    lower, upper = list(range(STEPS)), list(range(STEPS))
-    lower[OUTSIDE - 4 : OUTSIDE] = [ORDER.index(entry) for entry in [(-1, 0), (-1, 1), (1, 0), (1, 1)]]
-    upper[OUTSIDE - 4 : OUTSIDE] = [ORDER.index(entry) for entry in [(1, 0), (1, 1), (-1, 0), (-1, 1)]]
-    place = jnp.where((win > 0) & (win < WIN // 2), look_up(step, lower), step)
-    return jnp.where(win > WIN // 2, look_up(step, upper), place)
+def entry_of(step, win):
+    nearest = list(range(OUTSIDE - 4)) + [OUTSIDE - 2, OUTSIDE - 1, OUTSIDE - 4, OUTSIDE - 3, STEPS - 2, STEPS - 1]
+    second = list(range(OUTSIDE - 8)) + [OUTSIDE - 6, OUTSIDE - 5, OUTSIDE - 8, OUTSIDE - 7]
+    second += nearest[OUTSIDE - 4 :]
+    place = jnp.where((win == 1) | (win == 4), look_up(step, nearest), step)
+    return jnp.where(win == 2, look_up(step, second), place)
 
 
 def look_up(step, values):
@@ -92,12 +93,12 @@
     mates = [(first + lax.rem(place + k, ROW), win) for k in range(1, ROW)]
     partners = mates + [(above, win), (below, win)]
     beside = [(chan, after), (chan, before)]
-    odd = win % 2 == 1
+    greeted = look_up(win, GREETED)
     for partner in partners:
         pl.semaphore_signal(barrier, inc=1, device_id=partner, device_id_type=MESH)
 
     def trace_copy(i):
-        entry = toward_first(i, win)
+        entry = entry_of(i, win)
         target = lax.rem(win + look_up(entry, [(where + WIN) % WIN for where, _ in ORDER]), WIN)
         half = look_up(entry, [half for _, half in ORDER])
         rows = pl.ds(pl.multiple_of((2 * target + half) * PART, PART), PART)
@@ -153,34 +154,40 @@
                 for h in range(2):
                     share = slice(h * SHARE, (h + 1) * SHARE)
                     both = jnp.concatenate([re[share], im[share]], axis=0)
-                    white[i, 2 * g + h, s] = both.astype(jnp.bfloat16)
-
-    def send_row(i):
+                    white[i, s // (segments // CUTS), 2 * g + h, s % (segments // CUTS)] = both.astype(jnp.bfloat16)
+
+    def send_row(i, c):
         for k, mate in enumerate(mates):
             other = lax.rem(place + k + 1, ROW)
             pltpu.make_async_remote_copy(
-                white.at[i, other], got.at[i, HALO + place], xs.at[i], xr.at[i], device_id=mate, device_id_type=MESH
+                white.at[i, c, other],
+                got.at[i, c, HALO + place],
+                xs.at[i, c],
+                xr.at[i, c],
+                device_id=mate,
+                device_id_type=MESH,
             ).start()
-        got[i, HALO + place] = white[i, place]
-
-    def row_wait(i):
-        block = got.at[i, pl.ds(0, ROW - 1)]
-        return pltpu.make_async_remote_copy(block, block, xs.at[i], xr.at[i], device_id=mates[0], device_id_type=MESH)
-
-    def near_copy(i, source, target, device):
+
+    def row_wait(i, c):
+        block = got.at[i, c, pl.ds(0, ROW - 1)]
         return pltpu.make_async_remote_copy(
-            got.at[i, pl.ds(source, HALO)],
-            got.at[i, pl.ds(target, HALO)],
-            ys.at[i],
-            yr.at[i],
+            block, block, xs.at[i, c], xr.at[i, c], device_id=mates[0], device_id_type=MESH
+        )
+
+    def near_copy(i, c, source, target, device):
+        return pltpu.make_async_remote_copy(
+            got.at[i, c, pl.ds(source, HALO)],
+            got.at[i, c, pl.ds(target, HALO)],
+            ys.at[i, c],
+            yr.at[i, c],
             device_id=(device, win),
             device_id_type=MESH,
         )
 
-    def near_wait(i):
-        block = got.at[i, pl.ds(0, 2 * HALO)]
+    def near_wait(i, c):
+        block = got.at[i, c, pl.ds(0, 2 * HALO)]
         return pltpu.make_async_remote_copy(
-            block, block, ys.at[i], yr.at[i], device_id=(above, win), device_id_type=MESH
+            block, block, ys.at[i, c], yr.at[i, c], device_id=(above, win), device_id_type=MESH
         )
 
     def chain_copy(i):
@@ -192,7 +199,8 @@
 
     def cross(i):
         def move(b, carry):
-            near[b] = got[i, b]
+            for c in range(CUTS):
+                near[b, pl.ds(c * (segments // CUTS), segments // CUTS)] = got[i, c, b]
             return carry
 
         lax.fori_loop(0, ROW + 2 * HALO, move, 0, unroll=True)
@@ -235,8 +243,8 @@
         def _():
             half = i - OUTSIDE
             chain_copy(slot).wait_recv()
-            chain_copy(slot + 1).wait_recv()
-            total = part[...] + zin[slot].astype(jnp.float32) + zin[slot + 1].astype(jnp.float32)
+            chain_copy(slot - 2).wait_recv()
+            total = part[...] + zin[slot].astype(jnp.float32) + zin[slot - 2].astype(jnp.float32)
             fout[half] = total.astype(jnp.bfloat16)
             for k, mate in enumerate(mates):
                 other = lax.rem(place + k + 1, ROW)
@@ -259,24 +267,25 @@
     def step(n, carry):
         send, arrived, paired = n - 1, n - 1 - WINDOW, n - 1 - WINDOW - LAG
 
-        @pl.when((arrived >= 0) & (arrived < STEPS))
-        def _():
-            row_wait(arrived).wait_recv()
-
         @pl.when(send == 0)
         def _():
-            pl.semaphore_wait(barrier, len(partners) + jnp.where(odd, len(beside), 0))
+            pl.semaphore_wait(barrier, len(partners) + greeted)
             for partner in beside:
                 pl.semaphore_signal(barrier, inc=1, device_id=partner, device_id_type=MESH)
 
+        @pl.when((arrived >= 0) & (arrived < STEPS))
+        def _():
+            for c in range(CUTS):
+                row_wait(arrived, c).wait_recv()
+                near_copy(arrived, c, HALO, HALO + ROW, below).start()
+                near_copy(arrived, c, ROW, 0, above).start()
+
         @pl.when((send >= 0) & (send < STEPS))
         def _():
-            send_row(send)
-
-        @pl.when((arrived >= 0) & (arrived < STEPS))
-        def _():
-            near_copy(arrived, HALO, HALO + ROW, below).start()
-            near_copy(arrived, ROW, 0, above).start()
+            for c in range(CUTS):
+                send_row(send, c)
+            for c in range(CUTS):
+                got[send, c, HALO + place] = white[send, c, place]
 
         @pl.when(n < STEPS)
         def _():
@@ -287,15 +296,16 @@
             tables[3].wait()
             tables[4].wait()
 
-            @pl.when(jnp.logical_not(odd))
+            @pl.when(greeted < len(beside))
             def _():
-                pl.semaphore_wait(barrier, len(beside))
+                pl.semaphore_wait(barrier, len(beside) - greeted)
 
         @pl.when(paired >= 0)
         def _():
-            near_wait(paired).wait_recv()
+            for c in range(CUTS):
+                near_wait(paired, c).wait_recv()
             cross(paired)
-            add_up(toward_first(paired, win))
+            add_up(entry_of(paired, win))
 
         return carry
 
@@ -320,8 +330,9 @@
         final_wait(half).wait_send()
 
     def drain(i, carry):
-        row_wait(i).wait_send()
-        near_wait(i).wait_send()
+        for c in range(CUTS):
+            row_wait(i, c).wait_send()
+            near_wait(i, c).wait_send()
 
         @pl.when(i < OUTSIDE)
         def _():
@@ -341,6 +352,7 @@
     pairs = SLOTS * ROW
     tile = (2 * SHARE, LANES)
     block = (segments,) + tile
+    cut = (segments // CUTS,) + tile
     any_space, vmem = pl.BlockSpec(memory_space=pl.ANY), pl.BlockSpec(memory_space=pltpu.VMEM)
     dma = pltpu.SemaphoreType.DMA
     return pl.pallas_call(
@@ -361,8 +373,8 @@
             pltpu.VMEM((rows, bins), bf16),
             pltpu.VMEM((rows, bins), f32),
             pltpu.VMEM((rows, LANES), f32),
-            pltpu.VMEM((STEPS, ROW) + block, bf16),
-            pltpu.VMEM((STEPS, ROW + 2 * HALO) + block, bf16),
+            pltpu.VMEM((STEPS, CUTS, ROW) + cut, bf16),
+            pltpu.VMEM((STEPS, CUTS, ROW + 2 * HALO) + cut, bf16),
             pltpu.VMEM((ROW + 2 * HALO,) + block, bf16),
             pltpu.VMEM((pairs,) + tile, f32),
             pltpu.VMEM((OUTSIDE, pairs) + tile, bf16),
@@ -372,10 +384,10 @@
             pltpu.VMEM((SLOTS * PART, length), bf16),
             dma((5,)),
             dma((STEPS,)),
-            dma((STEPS,)),
-            dma((STEPS,)),
-            dma((STEPS,)),
-            dma((STEPS,)),
+            dma((STEPS, CUTS)),
+            dma((STEPS, CUTS)),
+            dma((STEPS, CUTS)),
+            dma((STEPS, CUTS)),
             dma((OUTSIDE,)),
             dma((OUTSIDE,)),
             dma((2,)),

time: 57.4 us -> 55.6 us (0.969)
  Pallas kernels: 55.5 us -> 53.7 us
    pallas_call x1, Pallas kernels: 55.5 us -> 53.7 us  [body(): pl.pallas_call(functools.partial(kernel, norm), out_shape=jax.ShapeDtypeS...]
where the time goes in v4:
time: 55.6 us; the launch traced here: 55.4 us
  Pallas kernels  53.7 us (97%)
  local copies, waits for them, and re-layouts  1.77 us (3%)
    pallas_call x1, Pallas kernels, body(): pl.pallas_call(functools.partial(kernel, norm), out_shape=jax.ShapeDtypeS...  53.7 us
    unnamed x1, local copies, waits for them, and re-layouts  1.77 us

profile of v4, /device:TPU:1, one launch (start us, length us, event | category | flops | bytes accessed | tf_op | source)
XLA Modules:
  0.0 55.4 jit_solution(7065839496301606349)
XLA Ops:
  0.0 53.7 %shard_map.64 = f32[3,32,1024]{2,1,0:T(8,128)} custom-call(s32[3,32]{1,0:T(4,128)} %bitcast.1, s32[32]{0:T(128)} %counts_in.1, bf16[6,256,1024]{2,1,0:T(8,128)(2,1)} %traces.1, bf16[1024,1024]{1,0:T(8,128)(2,1)} %constant.6.clone.forward, bf16[512,512]{1,0:T(8,128)(2,1)} %constant.7.clone.band, bf16[1024,1024]{1,0:T(8,128)(2,1)} %constant.8.clone.inverse), custom_call_target="tpu_custom_call" | custom-call | tf_op jit(solution)/shard_map/pallas_call | solution.py:358
  53.7 1.8 %copy.8 = f32[3,32,1024]{2,1,0:T(8,128)} copy(f32[3,32,1024]{2,1,0:T(8,128)} %shard_map.64) | data formatting | bytes 786432

commit v5 on v4

--- a/solution.py
+++ b/solution.py
@@ -20,7 +20,7 @@
 PART = 16
 SHARE = 8
 LANES = 128
-VMEM_BYTES = 62 << 20
+VMEM_BYTES = 107 << 19
 
 ORDER = [(where, half) for where in (-4, 3, -3, 2, -2, 1, -1, 0) for half in (0, 1)]
 STEPS = len(ORDER)
@@ -76,8 +76,8 @@
 
 
 def kernel(
-    norm, offsets_in, counts_in, traces, forward, band, inverse, out,
-    offsets, counts, tr, fwd, bnd, inv, weight, spec, high, low, smooth, water, white, got, near, part, zout, zin,
+    norm, pairs_in, traces, forward, band, inverse, out,
+    pairs, tr, fwd, bnd, inv, weight, spec, high, low, smooth, water, white, got, near, part, zout, zin,
     fout, fin, left, tab_sem, tr_sem, xs, xr, ys, yr, zs, zr, fs, fr,
 ):
     segments, bins = tr.shape[1], bnd.shape[0]
@@ -107,7 +107,7 @@
     tables = [
         pltpu.make_async_copy(source, target, tab_sem.at[k])
         for k, (source, target) in enumerate(
-            [(forward, fwd), (band, bnd), (inverse, inv), (offsets_in, offsets), (counts_in, counts)]
+            [(forward, fwd), (band, bnd), (inverse, inv), (pairs_in, pairs)]
         )
     ]
     tables[0].start()
@@ -208,8 +208,8 @@
         def owner(j, carry):
             source = [near[HALO + j, s].astype(jnp.float32) for s in range(segments)]
             for p in range(SLOTS):
-                receiver = HALO + j + offsets[p, first + j]
-                live = p < counts[first + j]
+                receiver = HALO + j + pairs[p, first + j]
+                live = p < pairs[SLOTS, first + j]
                 total_re = jnp.zeros((SHARE, LANES), jnp.float32)
                 total_im = jnp.zeros((SHARE, LANES), jnp.float32)
                 for s, both in enumerate(source):
@@ -294,7 +294,6 @@
         @pl.when(paired == 0)
         def _():
             tables[3].wait()
-            tables[4].wait()
 
             @pl.when(greeted < len(beside))
             def _():
@@ -310,6 +309,19 @@
         return carry
 
     lax.fori_loop(0, STEPS + 1 + WINDOW + LAG, step, 0)
+
+    def drain(i, carry):
+        for c in range(CUTS):
+            row_wait(i, c).wait_send()
+            near_wait(i, c).wait_send()
+
+        @pl.when(i < OUTSIDE)
+        def _():
+            chain_copy(i).wait_send()
+
+        return carry
+
+    lax.fori_loop(0, STEPS, drain, 0)
 
     tables[2].wait()
     for half in range(2):
@@ -328,19 +340,6 @@
 
     for half in range(2):
         final_wait(half).wait_send()
-
-    def drain(i, carry):
-        for c in range(CUTS):
-            row_wait(i, c).wait_send()
-            near_wait(i, c).wait_send()
-
-        @pl.when(i < OUTSIDE)
-        def _():
-            chain_copy(i).wait_send()
-
-        return carry
-
-    lax.fori_loop(0, STEPS, drain, 0)
 
 
 def body(traces, offsets, counts):
@@ -358,11 +357,10 @@
     return pl.pallas_call(
         functools.partial(kernel, norm),
         out_shape=jax.ShapeDtypeStruct((SLOTS, channels // WIN, length), f32),
-        in_specs=[any_space] * 6,
+        in_specs=[any_space] * 5,
         out_specs=vmem,
         scratch_shapes=[
-            pltpu.SMEM(offsets.shape[::-1], jnp.int32),
-            pltpu.SMEM(counts.shape, jnp.int32),
+            pltpu.SMEM((SLOTS + 1, counts.shape[0]), jnp.int32),
             pltpu.VMEM((STEPS, segments, PART, length), bf16),
             pltpu.VMEM((length, length), bf16),
             pltpu.VMEM((bins, bins), bf16),
@@ -382,7 +380,7 @@
             pltpu.VMEM((2, pairs) + tile, bf16),
             pltpu.VMEM((2, ROW, SLOTS) + tile, bf16),
             pltpu.VMEM((SLOTS * PART, length), bf16),
-            dma((5,)),
+            dma((4,)),
             dma((STEPS,)),
             dma((STEPS, CUTS)),
             dma((STEPS, CUTS)),
@@ -395,8 +393,7 @@
         ],
         compiler_params=pltpu.CompilerParams(collective_id=0, has_side_effects=True, vmem_limit_bytes=VMEM_BYTES),
     )(
-        offsets.T,
-        counts,
+        jnp.concatenate([offsets.T, counts[None]]),
         traces,
         jnp.asarray(forward_table(length)),
         jnp.asarray(band_table(bins)),

time: 55.6 us -> 54.3 us (0.977)
  local copies, waits for them, and re-layouts: 1.77 us -> 0.75 us
  Pallas kernels: 53.7 us -> 52.8 us
  other arithmetic: 0 us -> 0.71 us
    unnamed x1, local copies, waits for them, and re-layouts: 1.77 us -> 0.75 us
    pallas_call x1, Pallas kernels: 53.7 us -> 52.8 us  [body(): pl.pallas_call(functools.partial(kernel, norm), out_shape=jax.ShapeDtypeS...]
    concatenate x0 -> x1, other arithmetic: none -> 0.71 us  [body(): jnp.concatenate([offsets.T, counts[None]])]
where the time goes in v5:
time: 54.3 us; the launch traced here: 54.2 us
  Pallas kernels  52.8 us (97%)
  local copies, waits for them, and re-layouts  0.75 us (1%)
  other arithmetic  0.71 us (1%)
    pallas_call x1, Pallas kernels, body(): pl.pallas_call(functools.partial(kernel, norm), out_shape=jax.ShapeDtypeS...  52.8 us

profile of v5, /device:TPU:1, one launch (start us, length us, event | category | flops | bytes accessed | tf_op | source)
XLA Modules:
  0.0 54.2 jit_solution(7274589978870330785)
XLA Ops:
  0.0 0.7 %pad_add_fusion.pairs_in = s32[4,32]{1,0:T(4,128)S(1)} fusion(s32[1,32]{1,0:T(1,128)} %bitcast.3, s32[3,32]{1,0:T(4,128)} %bitcast.2), kind=kLoop, calls=%fused_computation | loop fusion | flops 128 | bytes 1024 | tf_op jit(solution)/shard_map/concatenate | solution.py:396
  0.7 52.8 %shard_map.64 = f32[3,32,1024]{2,1,0:T(8,128)S(1)} custom-call(s32[4,32]{1,0:T(4,128)S(1)} %pad_add_fusion.pairs_in, bf16[6,256,1024]{2,1,0:T(8,128)(2,1)} %traces.1, bf16[1024,1024]{1,0:T(8,128)(2,1)} %constant.6.clone.forward, bf16[512,512]{1,0:T(8,128)(2,1)} %constant.7.clone.band, bf16[1024,1024]{1,0:T(8,128)(2,1)} %constant.8.clone.inverse), custom_call_target="tpu_custom_call" | custom-call | tf_op jit(solution)/shard_map/pallas_call | solution.py:357
  53.5 0.7 %copy.8 = f32[3,32,1024]{2,1,0:T(8,128)} copy(f32[3,32,1024]{2,1,0:T(8,128)S(1)} %shard_map.64) | data formatting | bytes 786432

commit v6 on v5

--- a/solution.py
+++ b/solution.py
@@ -26,6 +26,7 @@
 STEPS = len(ORDER)
 OUTSIDE = STEPS - 2
 GREETED = [0, 1, 2, 0, 2, 0, 2, 1]
+FARTHEST_FIRST = [4, 3, 5, 2, 6, 1, 7]
 CUTS = 2
 WINDOW = 3
 LAG = 2
@@ -90,7 +91,7 @@
     after, before = lax.rem(win + 1, WIN), lax.rem(win + WIN - 1, WIN)
 
     barrier = pltpu.get_barrier_semaphore()
-    mates = [(first + lax.rem(place + k, ROW), win) for k in range(1, ROW)]
+    mates = [(first + lax.rem(place + k, ROW), win) for k in FARTHEST_FIRST]
     partners = mates + [(above, win), (below, win)]
     beside = [(chan, after), (chan, before)]
     greeted = look_up(win, GREETED)
@@ -158,7 +159,7 @@
 
     def send_row(i, c):
         for k, mate in enumerate(mates):
-            other = lax.rem(place + k + 1, ROW)
+            other = lax.rem(place + FARTHEST_FIRST[k], ROW)
             pltpu.make_async_remote_copy(
                 white.at[i, c, other],
                 got.at[i, c, HALO + place],
@@ -247,7 +248,7 @@
             total = part[...] + zin[slot].astype(jnp.float32) + zin[slot - 2].astype(jnp.float32)
             fout[half] = total.astype(jnp.bfloat16)
             for k, mate in enumerate(mates):
-                other = lax.rem(place + k + 1, ROW)
+                other = lax.rem(place + FARTHEST_FIRST[k], ROW)
                 pltpu.make_async_remote_copy(
                     fout.at[half, pl.ds(SLOTS * other, SLOTS)],
                     fin.at[half, place],

time: 54.3 us -> 54.1 us (level)
  no operation moved by 1% of the time
where the time goes in v6:
time: 54.1 us; the launch traced here: 54 us
  Pallas kernels  52.5 us (97%)
  local copies, waits for them, and re-layouts  0.75 us (1%)
  other arithmetic  0.71 us (1%)
    pallas_call x1, Pallas kernels, body(): pl.pallas_call(functools.partial(kernel, norm), out_shape=jax.ShapeDtypeS...  52.5 us

profile of v6, /device:TPU:1, one launch (start us, length us, event | category | flops | bytes accessed | tf_op | source)
XLA Modules:
  0.0 54.0 jit_solution(13215470116100222841)
XLA Ops:
  0.0 0.7 %pad_add_fusion.pairs_in = s32[4,32]{1,0:T(4,128)S(1)} fusion(s32[1,32]{1,0:T(1,128)} %bitcast.3, s32[3,32]{1,0:T(4,128)} %bitcast.2), kind=kLoop, calls=%fused_computation | loop fusion | flops 128 | bytes 1024 | tf_op jit(solution)/shard_map/concatenate | solution.py:397
  0.7 52.5 %shard_map.64 = f32[3,32,1024]{2,1,0:T(8,128)S(1)} custom-call(s32[4,32]{1,0:T(4,128)S(1)} %pad_add_fusion.pairs_in, bf16[6,256,1024]{2,1,0:T(8,128)(2,1)} %traces.1, bf16[1024,1024]{1,0:T(8,128)(2,1)} %constant.6.clone.forward, bf16[512,512]{1,0:T(8,128)(2,1)} %constant.7.clone.band, bf16[1024,1024]{1,0:T(8,128)(2,1)} %constant.8.clone.inverse), custom_call_target="tpu_custom_call" | custom-call | tf_op jit(solution)/shard_map/pallas_call | solution.py:358
  53.2 0.7 %copy.8 = f32[3,32,1024]{2,1,0:T(8,128)} copy(f32[3,32,1024]{2,1,0:T(8,128)S(1)} %shard_map.64) | data formatting | bytes 786432

commit v7 on v6

--- a/solution.py
+++ b/solution.py
@@ -65,6 +65,8 @@
     second = list(range(OUTSIDE - 8)) + [OUTSIDE - 6, OUTSIDE - 5, OUTSIDE - 8, OUTSIDE - 7]
     second += nearest[OUTSIDE - 4 :]
     place = jnp.where((win == 1) | (win == 4), look_up(step, nearest), step)
+    last = list(range(OUTSIDE - 6)) + [OUTSIDE - 4, OUTSIDE - 3, OUTSIDE - 6, OUTSIDE - 5] + list(range(OUTSIDE - 2, STEPS))
+    place = jnp.where(win == 7, look_up(step, last), place)
     return jnp.where(win == 2, look_up(step, second), place)
 
 

time: 54.1 us -> 54.1 us (level); the launches traced: 54 us -> 53.4 us
    pallas_call x1, Pallas kernels: 52.5 us -> 52 us  [body(): pl.pallas_call(functools.partial(kernel, norm), out_shape=jax.ShapeDtypeS...]
where the time goes in v7:
time: 54.1 us; the launch traced here: 53.4 us
  Pallas kernels  52 us (96%)
  local copies, waits for them, and re-layouts  0.75 us (1%)
  other arithmetic  0.71 us (1%)
    pallas_call x1, Pallas kernels, body(): pl.pallas_call(functools.partial(kernel, norm), out_shape=jax.ShapeDtypeS...  52 us

profile of v7, /device:TPU:1, one launch (start us, length us, event | category | flops | bytes accessed | tf_op | source)
XLA Modules:
  0.0 53.4 jit_solution(18427258496766805554)
XLA Ops:
  0.0 0.7 %pad_add_fusion.pairs_in = s32[4,32]{1,0:T(4,128)S(1)} fusion(s32[1,32]{1,0:T(1,128)} %bitcast.3, s32[3,32]{1,0:T(4,128)} %bitcast.2), kind=kLoop, calls=%fused_computation | loop fusion | flops 128 | bytes 1024 | tf_op jit(solution)/shard_map/concatenate | solution.py:399
  0.7 52.0 %shard_map.64 = f32[3,32,1024]{2,1,0:T(8,128)S(1)} custom-call(s32[4,32]{1,0:T(4,128)S(1)} %pad_add_fusion.pairs_in, bf16[6,256,1024]{2,1,0:T(8,128)(2,1)} %traces.1, bf16[1024,1024]{1,0:T(8,128)(2,1)} %constant.6.clone.forward, bf16[512,512]{1,0:T(8,128)(2,1)} %constant.7.clone.band, bf16[1024,1024]{1,0:T(8,128)(2,1)} %constant.8.clone.inverse), custom_call_target="tpu_custom_call" | custom-call | tf_op jit(solution)/shard_map/pallas_call | solution.py:360
  52.7 0.7 %copy.8 = f32[3,32,1024]{2,1,0:T(8,128)} copy(f32[3,32,1024]{2,1,0:T(8,128)S(1)} %shard_map.64) | data formatting | bytes 786432
